TPU v7x, 256 devices: a whole 4x4x8 slice. The times are simulated.
256 devices in a mesh: band: 8 (over x, core), dom: 32 (over z, y).
Axes of the slice: x: 4, y: 4, z: 8, core: 2. Of those that a mesh axis runs over, the one named last changes fastest.
Arguments:
- orbitals: bfloat16 [256, 192, 48, 64], P('band', 'dom'), may hold values from -1.796875 to 1.796875
- potential: float32 [192, 48, 64], P('dom'), may hold values from -2 to 1
- projectors: float32 [2048, 128], P('dom'), may hold values from -1.5 to 1.5
- coupling: float32 [1024], P('dom'), may hold values from 0.5 to 2
- slot_block: int32 [2048], P('dom'), may hold values from 0 to 143
- slot_projector: int32 [2048], P('dom'), may hold values from 0 to 1023, as said below
- slot_count: int32 [32], P('dom'), may hold values from 16 to 64, as said below
- locked: bfloat16 [2048, 192, 3072], P(None, 'dom', 'band'), may hold values from -0.0078125 to 0.0078125
Outputs:
- orthogonal: bfloat16 [256, 192, 3072], P(None, 'dom', 'band')
- margins: float32 [2048, 256], P(('band', 'dom'))
Inputs may be any that keep to these rules, and one draw needn't show every extreme that they name: `slot_projector`: projector p belongs to domain p // 32; a slot of domain d names a projector of domain d - 1, d or d + 1, cyclically; slot 0 of every domain names one of domain d - 1 and slot 1 one of domain d + 1. The used slots of a domain are its first slot_count slots; some domain uses all and some uses 64 // 4.
All inputs are finite; a program needn't handle non-finite values.
Results may differ from a plain program's by a relative error of at most 0.0039.
The roundings to bfloat16 on the way count: a program that leaves them out, or rounds other values in their place, can miss the bound.
Values may be sent and summed in bfloat16 or wider, within the bound.
No kernel may reach another device: no remote copies, remote signals or barrier semaphores. Data moves between devices by JAX's collectives and lax.ppermute only.
A program may use at most 320 MiB of HBM per device.

v0:
```python
import jax
import jax.numpy as jnp
from jax import lax
from jax.sharding import PartitionSpec as P

BS = 128
PROJ_DOM = 32
COEFFS = (
    -5369.0 / 1800.0,
    12.0 / 7.0,
    -15.0 / 56.0,
    10.0 / 189.0,
    -1.0 / 112.0,
    2.0 / 825.0,
    -1.0 / 5544.0,
)


def with_halo(shard, sides, width):
    for axis, dim in sides:
        size, length = (lax.axis_size(axis), shard.shape[dim])
        up = [(i, (i + 1) % size) for i in range(size)]
        down = [(j, i) for i, j in up]
        last = lax.slice_in_dim(shard, length - width, length, axis=dim)
        initial = lax.slice_in_dim(shard, 0, width, axis=dim)
        before = lax.ppermute(last, axis, up)
        after = lax.ppermute(initial, axis, down)
        shard = jnp.concatenate([before, shard, after], axis=dim)
    return shard


def laplacian(orbital, extended):
    planes_x = orbital.shape[1]
    depth_z = orbital.shape[2]
    laplace = 3.0 * COEFFS[0] * orbital
    padded = jnp.pad(orbital, ((0, 0), (0, 0), (6, 6), (0, 0)))
    for offset in range(1, 7):
        weight = COEFFS[offset]
        laplace = laplace + weight * (
            extended[:, 6 + offset : 6 + offset + planes_x]
            + extended[:, 6 - offset : 6 - offset + planes_x]
        )
        laplace = laplace + weight * (jnp.roll(orbital, offset, 3) + jnp.roll(orbital, -offset, 3))
        laplace = laplace + weight * (
            padded[:, :, 6 + offset : 6 + offset + depth_z]
            + padded[:, :, 6 - offset : 6 - offset + depth_z]
        )
    return laplace


def per_device(
    orbitals, potential, projectors, coupling, slot_block, slot_projector, slot_count, locked
):
    orbital = orbitals.astype(jnp.float32)
    extended = with_halo(orbitals, (("dom", 1),), 6).astype(jnp.float32)
    laplace = laplacian(orbital, extended)
    band_rows, planes_x, depth_z, width_y = orbital.shape
    blocks_count = planes_x * depth_z * width_y // BS
    flat = orbital.reshape(band_rows, blocks_count, BS)
    blocks = flat[:, slot_block]
    slots = slot_block.shape[0]
    active = (jnp.arange(slots, dtype=jnp.int32) < slot_count[0]).astype(jnp.float32)
    inner_part = jnp.sum(blocks * projectors[None], axis=2) * active[None]
    domains = lax.axis_size("dom")
    here = lax.axis_index("dom")
    owner = slot_projector // PROJ_DOM
    local_id = slot_projector % PROJ_DOM
    relative = (owner - here + domains) % domains
    column = jnp.where(
        relative == 0,
        PROJ_DOM + local_id,
        jnp.where(relative == 1, 2 * PROJ_DOM + local_id, local_id),
    )
    onehot = (column[:, None] == jnp.arange(3 * PROJ_DOM, dtype=jnp.int32)[None, :]).astype(
        jnp.float32
    )
    partial_value = jnp.dot(inner_part, onehot, precision=lax.Precision.HIGHEST)
    outgoing = jnp.concatenate(
        [partial_value[:, :PROJ_DOM], partial_value[:, 2 * PROJ_DOM :]], axis=1
    )
    arrived = with_halo(outgoing, (("dom", 1),), PROJ_DOM)
    owned = (
        partial_value[:, PROJ_DOM : 2 * PROJ_DOM] + arrived[:, :PROJ_DOM] + arrived[:, -PROJ_DOM:]
    )
    table_local = owned * coupling[None]
    table = with_halo(table_local, (("dom", 1),), PROJ_DOM)
    slot_value = jnp.dot(table, onehot.T, precision=lax.Precision.HIGHEST) * active[None]
    contribution = slot_value[:, :, None] * projectors[None]
    nonlocal_term = jnp.zeros_like(flat).at[:, slot_block].add(contribution).reshape(orbital.shape)
    hamilton = -0.5 * laplace + potential[None] * orbital + nonlocal_term
    numerator, denominator = lax.psum(
        (jnp.sum(orbital * hamilton, axis=(1, 2, 3)), jnp.sum(orbital * orbital, axis=(1, 2, 3))),
        "dom",
    )
    energy = numerator / denominator
    residual = (hamilton - energy[:, None, None, None] * orbital).astype(jnp.bfloat16)
    residual = residual.reshape(band_rows, planes_x, depth_z * width_y)
    moved = lax.all_to_all(residual, "band", split_axis=2, concat_axis=0, tiled=True)
    all_bands = moved.shape[0]
    locked_flat = locked.reshape(locked.shape[0], -1)
    residual_flat = moved.reshape(all_bands, -1)
    contract_cells = (((1,), (1,)), ((), ()))
    share_rows = locked.shape[0] // lax.axis_size(("band", "dom"))
    summed = lax.psum(
        lax.dot_general(
            locked_flat, residual_flat, contract_cells, preferred_element_type=jnp.float32
        ),
        ("band", "dom"),
    )
    margins = lax.dynamic_slice_in_dim(
        summed, lax.axis_index(("band", "dom")) * share_rows, share_rows, 0
    )
    coeffs = summed.astype(jnp.bfloat16)
    correction = lax.dot_general(
        coeffs, locked_flat, (((0,), (0,)), ((), ())), preferred_element_type=jnp.float32
    )
    orthogonal = (
        (residual_flat.astype(jnp.float32) - correction).astype(jnp.bfloat16).reshape(moved.shape)
    )
    return (orthogonal, margins)


def solution(mesh):
    in_specs = (
        P("band", "dom", None, None),
        P("dom", None, None),
        P("dom", None),
        P("dom"),
        P("dom"),
        P("dom"),
        P("dom"),
        P(None, "dom", "band"),
    )
    out_specs = (P(None, "dom", "band"), P(("band", "dom"), None))
    return jax.shard_map(
        per_device, mesh=mesh, in_specs=in_specs, out_specs=out_specs, check_vma=False
    )
```

profile of v0, /device:TPU:2, one launch (start us, length us, event | category | flops | bytes accessed | tf_op | source)
XLA Modules:
  0.0 610.1 jit_solution(6926809845291708726)
XLA Ops:
  8.8 6.8 %collective-permute-start.1 = (bf16[32,6,48,64]{3,2,1,0:T(8,128)(2,1)}, bf16[32,6,48,64]{3,2,1,0:T(8,128)(2,1)}, u32[]{:S(2)}, u32[]{:S(2)}) collective-permute-start(bf16[32,6,48,64]{3,2,1,0:T(8,128)(2,1)} %param.8), channel_id=1, source_target_pairs={{1,0},{2,1},{3,2},{4,3},{5,4},{6,5},{7,6},{8,7},{9,8},{10,9},{11,1... | collective-permute-start | bytes 3538952 | tf_op jit(solution)/shard_map/ppermute | solution.py:27
  27.8 5.8 collective-permute-start.3
  38.1 4.7 fusion.66
  42.8 4.7 fusion.67
  52.1 4.6 fusion.69
  61.3 4.7 fusion.71
  66.0 4.6 fusion.72
  75.2 4.7 fusion.74
  79.9 4.6 fusion.75
  84.7 5.5 collective-permute-start.5
  90.2 4.7 fusion.76
  99.9 8.0 %scatter_fusion = f32[32,144,128]{2,0,1:T(8,128)} fusion(f32[32,144,128]{2,0,1:T(8,128)} %broadcast_in_dim.4, s32[64]{0:T(128)S(1)} %compare_select_fusion, f32[64,32,128]{2,1,0:T(8,128)S(1)} %multiply_bitcast_fusion), kind=kCustom, calls=%fused_computation.1 | custom fusion | flops 262144 | bytes 3145984 | tf_op jit(solution)/shard_map/scatter-add | solution.py:89
  117.0 8.1 %maximum_convert_fusion = f32[32,18,48,64]{3,2,1,0:T(8,128)} fusion(bf16[32,6,48,64]{3,2,1,0:T(8,128)(2,1)} %collective-permute-done.1, bf16[32,6,48,64]{3,2,1,0:T(8,128)(2,1)S(1)} %copy-done, bf16[32,6,48,64]{3,2,1,0:T(8,128)(2,1)} %collective-permute-done), kind=kLoop, calls=%fused_computation.14 | loop fusion | flops 5308416 | bytes 10616832 | tf_op jit(solution)/shard_map/convert_element_type | solution.py:55
  125.1 75.7 %fusion.21 = (f32[32]{0:T(128)S(1)}, f32[32]{0:T(128)S(1)}, f32[32,6,48,64]{3,2,1,0:T(8,128)}) fusion(bf16[32,6,48,64]{3,2,1,0:T(8,128)(2,1)S(1)} %copy-done, f32[32,6,48,64]{3,2,1,0:T(8,128)} %reshape.35, f32[6,48,64]{2,1,0:T(8,128)S(1)} %copy-done.1, f32[32,6,48,6]{3,2,1,0:T(8,128)} %get-tuple-element.36, f32[32,6,48,58]{3,2,1,0:T(8,128)} %get-tuple-element.38, ...), kind=kLoop, calls=%fused_computation.41 | loop fusion | flops 44826560 | bytes 64954624 | tf_op jit(solution)/shard_map/reduce_sum | solution.py:92
  200.8 69.9 %all-reduce.1 = (f32[32]{0:T(128)S(1)}, f32[32]{0:T(128)S(1)}) all-reduce(f32[32]{0:T(128)S(1)} %get-tuple-element.11, f32[32]{0:T(128)S(1)} %get-tuple-element.10), channel_id=1, replica_groups=mesh['band'=8,'dom'=32] {'dom'}, use_global_device_ids=true, to_apply=%region_3.4 | all-reduce | flops 64 | bytes 512 | tf_op jit(solution)/shard_map/psum | solution.py:91
  275.2 7.8 %copy.45 = bf16[32,6,48,64]{0,1,3,2:T(8,128)(2,1)} copy(bf16[32,6,48,64]{3,2,1,0:T(8,128)(2,1)} %fusion.23) | data formatting | bytes 2359296 | tf_op jit(solution)/shard_map/reshape | solution.py:97
  283.0 8.6 %reshape.59 = bf16[8,2,36864]{2,1,0:T(2,128)(2,1)} reshape(bf16[3072,6,32]{2,1,0:T(8,128)(2,1)} %bitcast.23) | data formatting | bytes 2359296
  291.6 4.8 all-to-all-start
  296.5 12.5 %copy.37 = bf16[2048,6,384]{0,2,1:T(8,128)(2,1)} copy(bf16[2048,6,384]{2,0,1:T(8,128)(2,1)} %param.15) | data formatting | bytes 18874368 | tf_op args[7]
  312.4 6.2 %reshape.60 = bf16[3072,6,32]{2,1,0:T(8,128)(2,1)} reshape(bf16[8,2,36864]{2,1,0:T(2,128)(2,1)S(1)} %all-to-all-done) | data formatting | bytes 2359296
  318.5 6.5 %copy.36 = bf16[8,32,6,384]{3,2,1,0:T(8,128)(2,1)S(1)} copy(bf16[8,32,6,384]{1,2,3,0:T(8,128)(2,1)} %bitcast.24) | data formatting | bytes 2359296 | tf_op jit(solution)/shard_map/all_to_all | solution.py:98
  325.2 7.7 %convolution_bitcast_fusion = f32[2048,256]{0,1:T(8,128)} fusion(bf16[256,2304]{1,0:T(8,128)(2,1)S(1)} %bitcast.29, bf16[2048,2304]{0,1:T(8,128)(2,1)} %bitcast.25), kind=kOutput, calls=%fused_computation.82 | convolution fusion | flops 2415919104 | bytes 12713984 | tf_op jit(solution)/shard_map/dot_general | solution.py:105
  333.0 259.3 %all-reduce.4.cloned.1.call-done = f32[2048,256]{0,1:T(8,128)} async-done(((f32[2048,256]{0,1:T(8,128)}), f32[2048,256]{0,1:T(8,128)}) %all-reduce.4.cloned.1.call-update) | async-done | bytes 2097168 | tf_op jit(solution)/shard_map/psum | solution.py:104
  592.3 7.0 %fusion.48 = bf16[256,2304]{1,0:T(8,128)(2,1)S(1)} fusion(bf16[2048,2304]{0,1:T(8,128)(2,1)} %bitcast.26, bf16[256,2304]{1,0:T(8,128)(2,1)S(1)} %bitcast.30, f32[2048,256]{0,1:T(8,128)} %all-reduce.4.cloned.1.call-done), kind=kOutput, calls=%fused_computation.81 | convolution fusion | flops 2418212864 | bytes 13893632 | tf_op jit(solution)/shard_map/dot_general | solution.py:114
  (53 shorter events, 57.4 us)
Async XLA Ops:
  7.2 12.9 %copy-start.4 = (s32[64]{0:T(128)S(1)}, s32[64]{0:T(128)}, u32[]{:S(2)}) copy-start(s32[64]{0:T(128)} %param.12) | copy-start | bytes 772
  7.2 109.8 %collective-permute-start = (bf16[32,6,48,64]{3,2,1,0:T(8,128)(2,1)}, bf16[32,6,48,64]{3,2,1,0:T(8,128)(2,1)}, u32[]{:S(2)}, u32[]{:S(2)}) collective-permute-start(bf16[32,6,48,64]{3,2,1,0:T(8,128)(2,1)} %param.8), channel_id=1, source_target_pairs={{0,1},{1,2},{2,3},{3,4},{4,5},{5,6},{6,7},{7,8},{8,9},{9,10},{10,1... | collective-permute-start | bytes 3538952 | tf_op jit(solution)/shard_map/ppermute | solution.py:26
  8.8 108.2 %collective-permute-start.1 = (bf16[32,6,48,64]{3,2,1,0:T(8,128)(2,1)}, bf16[32,6,48,64]{3,2,1,0:T(8,128)(2,1)}, u32[]{:S(2)}, u32[]{:S(2)}) collective-permute-start(bf16[32,6,48,64]{3,2,1,0:T(8,128)(2,1)} %param.8), channel_id=1, source_target_pairs={{1,0},{2,1},{3,2},{4,3},{5,4},{6,5},{7,6},{8,7},{9,8},{10,9},{11,1... | collective-permute-start | bytes 3538952 | tf_op jit(solution)/shard_map/ppermute | solution.py:27
  15.7 9.1 %copy-start.5 = (s32[64]{0:T(128)S(1)}, s32[64]{0:T(128)}, u32[]{:S(2)}) copy-start(s32[64]{0:T(128)} %param.13) | copy-start | bytes 772
  15.7 11.4 %copy-start.2 = (f32[64,128]{1,0:T(8,128)S(1)}, f32[64,128]{1,0:T(8,128)}, u32[]{:S(2)}) copy-start(f32[64,128]{1,0:T(8,128)} %param.10) | copy-start | bytes 98308
  20.0 13.5 %copy-start = (bf16[32,6,48,64]{3,2,1,0:T(8,128)(2,1)S(1)}, bf16[32,6,48,64]{3,2,1,0:T(8,128)(2,1)}, u32[]{:S(2)}) copy-start(bf16[32,6,48,64]{3,2,1,0:T(8,128)(2,1)} %param.8) | copy-start | bytes 3538948
  27.7 56.8 %collective-permute-start.2 = (f32[32,32]{1,0:T(8,128)S(1)}, f32[32,32]{1,0:T(8,128)S(1)}, u32[]{:S(2)}, u32[]{:S(2)}) collective-permute-start(f32[32,32]{1,0:T(8,128)S(1)} %get-tuple-element.39), channel_id=1, source_target_pairs={{0,1},{1,2},{2,3},{3,4},{4,5},{5,6},{6,7},{7,8},{8,9},{9,10},{10,1... | collective-permute-start | bytes 12296 | tf_op jit(solution)/shard_map/ppermute | solution.py:26
  27.8 56.8 %collective-permute-start.3 = (f32[32,32]{1,0:T(8,128)S(1)}, f32[32,32]{1,0:T(8,128)S(1)}, u32[]{:S(2)}, u32[]{:S(2)}) collective-permute-start(f32[32,32]{1,0:T(8,128)S(1)} %get-tuple-element.40), channel_id=1, source_target_pairs={{1,0},{2,1},{3,2},{4,3},{5,4},{6,5},{7,6},{8,7},{9,8},{10,9},{11,1... | collective-permute-start | bytes 12296 | tf_op jit(solution)/shard_map/ppermute | solution.py:27
  79.9 4.7 copy-start.3
  84.6 12.9 %collective-permute-start.4 = (f32[32,32]{1,0:T(8,128)S(1)}, f32[32,32]{1,0:T(8,128)S(1)}, u32[]{:S(2)}, u32[]{:S(2)}) collective-permute-start(f32[32,32]{1,0:T(8,128)S(1)} %fusion.53), channel_id=1, source_target_pairs={{0,1},{1,2},{2,3},{3,4},{4,5},{5,6},{6,7},{7,8},{8,9},{9,10},{10,1... | collective-permute-start | bytes 12296 | tf_op jit(solution)/shard_map/ppermute | solution.py:26
  84.7 12.9 %collective-permute-start.5 = (f32[32,32]{1,0:T(8,128)S(1)}, f32[32,32]{1,0:T(8,128)S(1)}, u32[]{:S(2)}, u32[]{:S(2)}) collective-permute-start(f32[32,32]{1,0:T(8,128)S(1)} %fusion.53), channel_id=1, source_target_pairs={{1,0},{2,1},{3,2},{4,3},{5,4},{6,5},{7,6},{8,7},{9,8},{10,9},{11,1... | collective-permute-start | bytes 12296 | tf_op jit(solution)/shard_map/ppermute | solution.py:27
  117.0 8.1 %copy-start.1 = (f32[6,48,64]{2,1,0:T(8,128)S(1)}, f32[6,48,64]{2,1,0:T(8,128)}, u32[]{:S(2)}) copy-start(f32[6,48,64]{2,1,0:T(8,128)} %param.9) | copy-start | bytes 221188
  291.6 20.7 %all-to-all-start = ((bf16[8,2,36864]{2,1,0:T(2,128)(2,1)}), bf16[8,2,36864]{2,1,0:T(2,128)(2,1)S(1)}, u32[]{:S(2)}, u32[]{:S(2)}) async-start(bf16[8,2,36864]{2,1,0:T(2,128)(2,1)} %reshape.59), calls=%async_computation | async-start | bytes 2359296 | tf_op jit(solution)/shard_map/all_to_all | solution.py:98
  296.5 295.9 %all-reduce.4.cloned.1.call-start = ((), (), s32[]{:S(2)}) async-start(), calls=%async_computation.1 | async-start | bytes 4194304 | tf_op jit(solution)/shard_map/psum | solution.py:104
Sparse Core Ops, SparseCore 0:
  333.1 259.1 all-reduce.3
where the time goes:
time: 616 us; the launch traced here: 610 us
  waiting for transfers between devices  263 us (43%)
  local copies, waits for them, and re-layouts  123 us (20%)
  other arithmetic  99.9 us (16%)
  blocking collectives  69.9 us (11%)
  starting transfers between devices  24.7 us (4%)
  matrix products  15.2 us (2%)
  between operations  15.1 us (2%)
    psum x1, waiting for transfers between devices, per_device(): lax.psum(lax.dot_general(locked_flat, residual_flat, contract_cells, pref...  259 us
    reduce_sum x1, other arithmetic, per_device(): jnp.sum(orbital * orbital, axis=(1, 2, 3))  75.7 us
    psum x1, blocking collectives, per_device(): lax.psum((jnp.sum(orbital * hamilton, axis=(1, 2, 3)), jnp.sum(orbital *...  69.9 us
    slice x12, local copies, waits for them, and re-layouts, laplacian(): jnp.roll(orbital, offset, 3) + jnp.roll(orbital, -offset, 3)  55.6 us
    unnamed x18, local copies, waits for them, and re-layouts  29.6 us
    ppermute x3, starting transfers between devices, with_halo(): after = lax.ppermute(initial, axis, down)  18.1 us
  transfers between devices with their start and end apart: 8, of which 2 were waited for; matrix products, arithmetic and copies ran while one was open for 17% of the time, Pallas kernels for 0%

commit v1 on v0

--- a/solution.py
+++ b/solution.py
@@ -102,10 +102,13 @@
     contract_cells = (((1,), (1,)), ((), ()))
     share_rows = locked.shape[0] // lax.axis_size(("band", "dom"))
     summed = lax.psum(
-        lax.dot_general(
-            locked_flat, residual_flat, contract_cells, preferred_element_type=jnp.float32
+        lax.psum(
+            lax.dot_general(
+                locked_flat, residual_flat, contract_cells, preferred_element_type=jnp.float32
+            ),
+            "dom",
         ),
-        ("band", "dom"),
+        "band",
     )
     margins = lax.dynamic_slice_in_dim(
         summed, lax.axis_index(("band", "dom")) * share_rows, share_rows, 0

time: 616 us -> 579 us (0.940)
  waiting for transfers between devices: 263 us -> 223 us
    psum x1, waiting for transfers between devices: 259 us -> 152 us  [per_device(): lax.psum(lax.dot_general(locked_flat, residual_flat, contract_cells, pref...]
    psum x0 -> x1, waiting for transfers between devices: none -> 67.7 us  [per_device(): lax.psum(lax.psum(lax.dot_general(locked_flat, residual_flat, contract_ce...]
  transfers between devices with their start and end apart: 8 -> 9, of which waited for: 2 -> 3; matrix products, arithmetic and copies ran while one was open for 17% -> 18% of each run, Pallas kernels for 0% -> 0%
where the time goes in v1:
time: 579 us; the launch traced here: 571 us
  waiting for transfers between devices  223 us (39%)
  local copies, waits for them, and re-layouts  123 us (21%)
  other arithmetic  99.9 us (17%)
  blocking collectives  69.9 us (12%)
  starting transfers between devices  24.7 us (4%)
  matrix products  15.2 us (3%)
  between operations  15.1 us (3%)
    psum x1, waiting for transfers between devices, per_device(): lax.psum(lax.dot_general(locked_flat, residual_flat, contract_cells, pref...  152 us
    reduce_sum x1, other arithmetic, per_device(): jnp.sum(orbital * orbital, axis=(1, 2, 3))  75.7 us
    psum x1, blocking collectives, per_device(): lax.psum((jnp.sum(orbital * hamilton, axis=(1, 2, 3)), jnp.sum(orbital *...  69.9 us
    psum x1, waiting for transfers between devices, per_device(): lax.psum(lax.psum(lax.dot_general(locked_flat, residual_flat, contract_ce...  67.7 us
    slice x12, local copies, waits for them, and re-layouts, laplacian(): jnp.roll(orbital, offset, 3) + jnp.roll(orbital, -offset, 3)  55.6 us
    unnamed x18, local copies, waits for them, and re-layouts  29.6 us
    ppermute x3, starting transfers between devices, with_halo(): after = lax.ppermute(initial, axis, down)  18.1 us
  transfers between devices with their start and end apart: 9, of which 3 were waited for; matrix products, arithmetic and copies ran while one was open for 18% of the time, Pallas kernels for 0%

profile of v1, /device:TPU:2, one launch (start us, length us, event | category | flops | bytes accessed | tf_op | source)
XLA Modules:
  0.0 570.7 jit_solution(17742313811567750889)
XLA Ops:
  8.8 6.8 %collective-permute-start.1 = (bf16[32,6,48,64]{3,2,1,0:T(8,128)(2,1)}, bf16[32,6,48,64]{3,2,1,0:T(8,128)(2,1)}, u32[]{:S(2)}, u32[]{:S(2)}) collective-permute-start(bf16[32,6,48,64]{3,2,1,0:T(8,128)(2,1)} %param.8), channel_id=1, source_target_pairs={{1,0},{2,1},{3,2},{4,3},{5,4},{6,5},{7,6},{8,7},{9,8},{10,9},{11,1... | collective-permute-start | bytes 3538952 | tf_op jit(solution)/shard_map/ppermute | solution.py:27
  27.8 5.8 %collective-permute-start.3 = (f32[32,32]{1,0:T(8,128)S(1)}, f32[32,32]{1,0:T(8,128)S(1)}, u32[]{:S(2)}, u32[]{:S(2)}) collective-permute-start(f32[32,32]{1,0:T(8,128)S(1)} %get-tuple-element.40), channel_id=1, source_target_pairs={{1,0},{2,1},{3,2},{4,3},{5,4},{6,5},{7,6},{8,7},{9,8},{10,9},{11,1... | collective-permute-start | bytes 12296 | tf_op jit(solution)/shard_map/ppermute | solution.py:27
  38.1 4.7 fusion.66
  42.8 4.7 fusion.67
  52.1 4.6 fusion.69
  61.3 4.7 fusion.71
  75.2 4.7 fusion.74
  79.9 4.6 fusion.75
  84.7 5.5 collective-permute-start.5
  90.2 4.7 fusion.76
  99.9 8.0 %scatter_fusion = f32[32,144,128]{2,0,1:T(8,128)} fusion(f32[32,144,128]{2,0,1:T(8,128)} %broadcast_in_dim.4, s32[64]{0:T(128)S(1)} %compare_select_fusion, f32[64,32,128]{2,1,0:T(8,128)S(1)} %multiply_bitcast_fusion), kind=kCustom, calls=%fused_computation.1 | custom fusion | flops 262144 | bytes 3145984 | tf_op jit(solution)/shard_map/scatter-add | solution.py:89
  117.0 8.1 %maximum_convert_fusion = f32[32,18,48,64]{3,2,1,0:T(8,128)} fusion(bf16[32,6,48,64]{3,2,1,0:T(8,128)(2,1)} %collective-permute-done.1, bf16[32,6,48,64]{3,2,1,0:T(8,128)(2,1)S(1)} %copy-done, bf16[32,6,48,64]{3,2,1,0:T(8,128)(2,1)} %collective-permute-done), kind=kLoop, calls=%fused_computation.14 | loop fusion | flops 5308416 | bytes 10616832 | tf_op jit(solution)/shard_map/convert_element_type | solution.py:55
  125.1 75.7 %fusion.21 = (f32[32]{0:T(128)S(1)}, f32[32]{0:T(128)S(1)}, f32[32,6,48,64]{3,2,1,0:T(8,128)}) fusion(bf16[32,6,48,64]{3,2,1,0:T(8,128)(2,1)S(1)} %copy-done, f32[32,6,48,64]{3,2,1,0:T(8,128)} %reshape.35, f32[6,48,64]{2,1,0:T(8,128)S(1)} %copy-done.1, f32[32,6,48,6]{3,2,1,0:T(8,128)} %get-tuple-element.36, f32[32,6,48,58]{3,2,1,0:T(8,128)} %get-tuple-element.38, ...), kind=kLoop, calls=%fused_computation.41 | loop fusion | flops 44826560 | bytes 64954624 | tf_op jit(solution)/shard_map/reduce_sum | solution.py:92
  200.8 69.9 %all-reduce.1 = (f32[32]{0:T(128)S(1)}, f32[32]{0:T(128)S(1)}) all-reduce(f32[32]{0:T(128)S(1)} %get-tuple-element.11, f32[32]{0:T(128)S(1)} %get-tuple-element.10), channel_id=1, replica_groups=mesh['band'=8,'dom'=32] {'dom'}, use_global_device_ids=true, to_apply=%region_3.4 | all-reduce | flops 64 | bytes 512 | tf_op jit(solution)/shard_map/psum | solution.py:91
  275.2 7.8 %copy.45 = bf16[32,6,48,64]{0,1,3,2:T(8,128)(2,1)} copy(bf16[32,6,48,64]{3,2,1,0:T(8,128)(2,1)} %fusion.23) | data formatting | bytes 2359296 | tf_op jit(solution)/shard_map/reshape | solution.py:97
  283.0 8.6 %reshape.59 = bf16[8,2,36864]{2,1,0:T(2,128)(2,1)} reshape(bf16[3072,6,32]{2,1,0:T(8,128)(2,1)} %bitcast.23) | data formatting | bytes 2359296
  291.6 4.8 all-to-all-start
  296.5 12.5 %copy.37 = bf16[2048,6,384]{0,2,1:T(8,128)(2,1)} copy(bf16[2048,6,384]{2,0,1:T(8,128)(2,1)} %param.15) | data formatting | bytes 18874368 | tf_op args[7]
  312.4 6.2 %reshape.60 = bf16[3072,6,32]{2,1,0:T(8,128)(2,1)} reshape(bf16[8,2,36864]{2,1,0:T(2,128)(2,1)S(1)} %all-to-all-done) | data formatting | bytes 2359296
  318.5 6.5 %copy.36 = bf16[8,32,6,384]{3,2,1,0:T(8,128)(2,1)S(1)} copy(bf16[8,32,6,384]{1,2,3,0:T(8,128)(2,1)} %bitcast.24) | data formatting | bytes 2359296 | tf_op jit(solution)/shard_map/all_to_all | solution.py:98
  325.2 7.7 %convolution_bitcast_fusion = f32[2048,256]{0,1:T(8,128)} fusion(bf16[256,2304]{1,0:T(8,128)(2,1)S(1)} %bitcast.29, bf16[2048,2304]{0,1:T(8,128)(2,1)} %bitcast.25), kind=kOutput, calls=%fused_computation.82 | convolution fusion | flops 2415919104 | bytes 12713984 | tf_op jit(solution)/shard_map/dot_general | solution.py:106
  333.1 152.2 %all-reduce.5.cloned.1.call-done = f32[2048,256]{0,1:T(8,128)} async-done(((f32[2048,256]{0,1:T(8,128)}), f32[2048,256]{0,1:T(8,128)}) %all-reduce.5.cloned.1.call-update) | async-done | bytes 2097168 | tf_op jit(solution)/shard_map/psum | solution.py:105
  485.3 67.7 %all-reduce.7.cloned.1.call-done = f32[2048,256]{0,1:T(8,128)} async-done(((f32[2048,256]{0,1:T(8,128)}), f32[2048,256]{0,1:T(8,128)}) %all-reduce.7.cloned.1.call-update) | async-done | bytes 2097168 | tf_op jit(solution)/shard_map/psum | solution.py:104
  552.9 7.0 %fusion.48 = bf16[256,2304]{1,0:T(8,128)(2,1)S(1)} fusion(bf16[2048,2304]{0,1:T(8,128)(2,1)} %bitcast.26, bf16[256,2304]{1,0:T(8,128)(2,1)S(1)} %bitcast.30, f32[2048,256]{0,1:T(8,128)} %all-reduce.7.cloned.1.call-done), kind=kOutput, calls=%fused_computation.81 | convolution fusion | flops 2418212864 | bytes 13893632 | tf_op jit(solution)/shard_map/dot_general | solution.py:117
  (56 shorter events, 62.1 us)
Async XLA Ops:
  7.2 12.9 %copy-start.4 = (s32[64]{0:T(128)S(1)}, s32[64]{0:T(128)}, u32[]{:S(2)}) copy-start(s32[64]{0:T(128)} %param.12) | copy-start | bytes 772
  7.2 109.8 %collective-permute-start = (bf16[32,6,48,64]{3,2,1,0:T(8,128)(2,1)}, bf16[32,6,48,64]{3,2,1,0:T(8,128)(2,1)}, u32[]{:S(2)}, u32[]{:S(2)}) collective-permute-start(bf16[32,6,48,64]{3,2,1,0:T(8,128)(2,1)} %param.8), channel_id=1, source_target_pairs={{0,1},{1,2},{2,3},{3,4},{4,5},{5,6},{6,7},{7,8},{8,9},{9,10},{10,1... | collective-permute-start | bytes 3538952 | tf_op jit(solution)/shard_map/ppermute | solution.py:26
  8.8 108.2 %collective-permute-start.1 = (bf16[32,6,48,64]{3,2,1,0:T(8,128)(2,1)}, bf16[32,6,48,64]{3,2,1,0:T(8,128)(2,1)}, u32[]{:S(2)}, u32[]{:S(2)}) collective-permute-start(bf16[32,6,48,64]{3,2,1,0:T(8,128)(2,1)} %param.8), channel_id=1, source_target_pairs={{1,0},{2,1},{3,2},{4,3},{5,4},{6,5},{7,6},{8,7},{9,8},{10,9},{11,1... | collective-permute-start | bytes 3538952 | tf_op jit(solution)/shard_map/ppermute | solution.py:27
  15.7 9.1 %copy-start.5 = (s32[64]{0:T(128)S(1)}, s32[64]{0:T(128)}, u32[]{:S(2)}) copy-start(s32[64]{0:T(128)} %param.13) | copy-start | bytes 772
  15.7 11.4 %copy-start.2 = (f32[64,128]{1,0:T(8,128)S(1)}, f32[64,128]{1,0:T(8,128)}, u32[]{:S(2)}) copy-start(f32[64,128]{1,0:T(8,128)} %param.10) | copy-start | bytes 98308
  20.0 13.5 %copy-start = (bf16[32,6,48,64]{3,2,1,0:T(8,128)(2,1)S(1)}, bf16[32,6,48,64]{3,2,1,0:T(8,128)(2,1)}, u32[]{:S(2)}) copy-start(bf16[32,6,48,64]{3,2,1,0:T(8,128)(2,1)} %param.8) | copy-start | bytes 3538948
  27.7 56.8 %collective-permute-start.2 = (f32[32,32]{1,0:T(8,128)S(1)}, f32[32,32]{1,0:T(8,128)S(1)}, u32[]{:S(2)}, u32[]{:S(2)}) collective-permute-start(f32[32,32]{1,0:T(8,128)S(1)} %get-tuple-element.39), channel_id=1, source_target_pairs={{0,1},{1,2},{2,3},{3,4},{4,5},{5,6},{6,7},{7,8},{8,9},{9,10},{10,1... | collective-permute-start | bytes 12296 | tf_op jit(solution)/shard_map/ppermute | solution.py:26
  27.8 56.8 %collective-permute-start.3 = (f32[32,32]{1,0:T(8,128)S(1)}, f32[32,32]{1,0:T(8,128)S(1)}, u32[]{:S(2)}, u32[]{:S(2)}) collective-permute-start(f32[32,32]{1,0:T(8,128)S(1)} %get-tuple-element.40), channel_id=1, source_target_pairs={{1,0},{2,1},{3,2},{4,3},{5,4},{6,5},{7,6},{8,7},{9,8},{10,9},{11,1... | collective-permute-start | bytes 12296 | tf_op jit(solution)/shard_map/ppermute | solution.py:27
  79.9 4.7 copy-start.3
  84.6 12.9 %collective-permute-start.4 = (f32[32,32]{1,0:T(8,128)S(1)}, f32[32,32]{1,0:T(8,128)S(1)}, u32[]{:S(2)}, u32[]{:S(2)}) collective-permute-start(f32[32,32]{1,0:T(8,128)S(1)} %fusion.53), channel_id=1, source_target_pairs={{0,1},{1,2},{2,3},{3,4},{4,5},{5,6},{6,7},{7,8},{8,9},{9,10},{10,1... | collective-permute-start | bytes 12296 | tf_op jit(solution)/shard_map/ppermute | solution.py:26
  84.7 12.9 %collective-permute-start.5 = (f32[32,32]{1,0:T(8,128)S(1)}, f32[32,32]{1,0:T(8,128)S(1)}, u32[]{:S(2)}, u32[]{:S(2)}) collective-permute-start(f32[32,32]{1,0:T(8,128)S(1)} %fusion.53), channel_id=1, source_target_pairs={{1,0},{2,1},{3,2},{4,3},{5,4},{6,5},{7,6},{8,7},{9,8},{10,9},{11,1... | collective-permute-start | bytes 12296 | tf_op jit(solution)/shard_map/ppermute | solution.py:27
  117.0 8.1 %copy-start.1 = (f32[6,48,64]{2,1,0:T(8,128)S(1)}, f32[6,48,64]{2,1,0:T(8,128)}, u32[]{:S(2)}) copy-start(f32[6,48,64]{2,1,0:T(8,128)} %param.9) | copy-start | bytes 221188
  291.6 20.7 %all-to-all-start = ((bf16[8,2,36864]{2,1,0:T(2,128)(2,1)}), bf16[8,2,36864]{2,1,0:T(2,128)(2,1)S(1)}, u32[]{:S(2)}, u32[]{:S(2)}) async-start(bf16[8,2,36864]{2,1,0:T(2,128)(2,1)} %reshape.59), calls=%async_computation | async-start | bytes 2359296 | tf_op jit(solution)/shard_map/all_to_all | solution.py:98
  296.5 188.8 %all-reduce.5.cloned.1.call-start = ((), (), s32[]{:S(2)}) async-start(), calls=%async_computation.1 | async-start | bytes 4194304 | tf_op jit(solution)/shard_map/psum | solution.py:105
  333.0 219.9 %all-reduce.7.cloned.1.call-start = ((), (), s32[]{:S(2)}) async-start(), calls=%async_computation.2 | async-start | bytes 4194304 | tf_op jit(solution)/shard_map/psum | solution.py:104
Sparse Core Ops, SparseCore 0:
  333.1 152.0 all-reduce.4
  487.7 65.1 all-reduce.6
